TPU v7x, 128 devices: a whole 4x4x4 slice. The times are simulated.
128 devices in a mesh: dp: 32 (over y, z, x_hi), tensor: 4 (over x_lo, core).
Axes of the slice: x: 4 (x_hi: 2, x_lo: 2; x = x_hi * 2 + x_lo), y: 4, z: 4, core: 2. Of those that a mesh axis runs over, the one named last changes fastest.
Arguments:
- tokens: bfloat16 [65536, 512], P(('dp', 'tensor')), may hold values from -6 to 6
- cotangent: bfloat16 [65536, 512], P(('dp', 'tensor')), may hold values from -6 to 6
- doc_lengths: int32 [32, 9], P('dp'), may hold values from 0 to 2048, as said below
- group_slot: int32 [128, 512], P(('dp', 'tensor')), may hold values from 0 to 511, each once within a row
- norm1_gain: float32 [512], replicated, may hold values from 0.5 to 1.5
- qkv_weight: bfloat16 [512, 1536], P(None, 'tensor'), may hold values from -0.25 to 0.25
- out_weight: bfloat16 [512, 512], P('tensor'), may hold values from -4 to 4
- norm2_gain: float32 [512], replicated, may hold values from 0.5 to 1.5
- router_weight: bfloat16 [512, 8], replicated, may hold values from -0.1875 to 0.1875
- expert_in: bfloat16 [8, 512, 2048], P('tensor'), may hold values from -1.5 to 1.5
- expert_out: bfloat16 [8, 2048, 512], P('tensor'), may hold values from -2 to 2
Outputs:
- block_out: bfloat16 [65536, 512], P(('dp', 'tensor'))
- grad_tokens: bfloat16 [65536, 512], P(('dp', 'tensor'))
- grad_norm1: float32 [512], replicated
- grad_qkv: float32 [512, 1536], P(None, 'tensor')
- grad_out: float32 [512, 512], P('tensor')
- grad_norm2: float32 [512], replicated
- grad_router: float32 [512, 8], replicated
- grad_expert_in: float32 [8, 512, 2048], P('tensor')
- grad_expert_out: float32 [8, 2048, 512], P('tensor')
Inputs may be any that keep to these rules, and one draw needn't show every extreme that they name: `doc_lengths`: each row's entries sum to 2048; a zero is an unused slot; documents fill the row in slot order.
All inputs are finite; a program needn't handle non-finite values.
Results may differ from a plain program's by a relative error of at most 0.035.
Values may be sent and summed in bfloat16 or wider, within the bound.
A program may use at most 128 MiB of HBM per device.

v0:
```python
from functools import partial

import jax
import jax.numpy as jnp
from jax import lax
from jax.sharding import PartitionSpec as P

D = 512
HEADS = 8
GROUP = 32


eps = 1e-06


def normalize(values):
    factor = lax.rsqrt(jnp.mean(values * values, axis=-1, keepdims=True) + eps)
    return (values * factor, factor)


def norm_back(grad_hidden, normed, factor, gain_row):
    grad_normed = grad_hidden * gain_row
    inner_sum = jnp.mean(grad_normed * normed, axis=-1, keepdims=True)
    return factor * (grad_normed - normed * inner_sum)


def block_scores(query_rows, all_keys, offset, block_rows, doc_ids, places, factor):
    query_docs = lax.dynamic_slice_in_dim(doc_ids, offset, block_rows, 0)
    query_places = lax.dynamic_slice_in_dim(places, offset, block_rows, 0)
    scores = (
        jnp.einsum("qhd,khd->hqk", query_rows, all_keys, preferred_element_type=jnp.float32)
        * factor
    )
    allowed = (query_docs[:, None] == doc_ids[None, :]) & (places[None, :] <= query_places[:, None])
    return jnp.where(allowed[None], scores, -1e30)


def local(
    tokens,
    cotangent,
    doc_lengths,
    group_slot,
    norm1_gain,
    qkv_weight,
    out_weight,
    norm2_gain,
    router_weight,
    expert_in,
    expert_out,
):
    data_ranks = lax.axis_size("dp")
    tensor_size = lax.axis_size("tensor")
    tok_rows = tokens.shape[0]
    length_all = tok_rows * tensor_size
    head_size = D // HEADS
    local_heads = qkv_weight.shape[1] // (3 * head_size)
    groups_here = tok_rows // GROUP
    per_source = GROUP // data_ranks
    experts_here = expert_in.shape[0]
    experts_all = router_weight.shape[1]
    factor = head_size ** (-0.5)
    block_rows = min(512, length_all)
    block_count = length_all // block_rows
    offsets = jnp.arange(block_count, dtype=jnp.int32) * block_rows
    contract_first = (((0,), (0,)), ((), ()))
    contract_last = (((1,), (1,)), ((), ()))
    inputs = tokens.astype(jnp.float32)
    normed_one, scale_one = normalize(inputs)
    hidden_one = (normed_one * norm1_gain).astype(jnp.bfloat16)
    rows_one = lax.all_gather(hidden_one, "tensor", axis=0, tiled=True)
    projected = jnp.dot(rows_one, qkv_weight, preferred_element_type=jnp.float32).astype(
        jnp.bfloat16
    )
    split_heads = projected.reshape(length_all, local_heads, 3, head_size)
    queries = split_heads[:, :, 0]
    all_keys = split_heads[:, :, 1]
    all_values = split_heads[:, :, 2]
    places = jnp.arange(length_all, dtype=jnp.int32)
    bounds = jnp.cumsum(doc_lengths[0])
    doc_ids = jnp.sum((places[:, None] >= bounds[None, :]).astype(jnp.int32), axis=1)

    def attend_block(offset):
        query_rows = lax.dynamic_slice_in_dim(queries, offset, block_rows, 0)
        scores = block_scores(query_rows, all_keys, offset, block_rows, doc_ids, places, factor)
        maxima = jnp.max(scores, axis=-1, keepdims=True)
        exponent = jnp.exp(scores - maxima)
        totals = jnp.sum(exponent, axis=-1, keepdims=True)
        weights = (exponent / totals).astype(jnp.bfloat16)
        attended = jnp.einsum(
            "hqk,khd->qhd", weights, all_values, preferred_element_type=jnp.float32
        )
        return (attended, (maxima + jnp.log(totals))[:, :, 0])

    attended_blocks, log_totals = lax.map(attend_block, offsets)
    attn_low = attended_blocks.reshape(length_all, local_heads * head_size).astype(jnp.bfloat16)
    attn_part = lax.psum_scatter(
        jnp.dot(attn_low, out_weight, preferred_element_type=jnp.float32).astype(jnp.bfloat16),
        "tensor",
        scatter_dimension=0,
        tiled=True,
    ).astype(jnp.float32)
    residual_one = inputs + attn_part
    normed_two, scale_two = normalize(residual_one)
    hidden_two = (normed_two * norm2_gain).astype(jnp.bfloat16)
    slot_row = group_slot[0]
    inverse_order = (
        jnp.zeros((tok_rows,), jnp.int32).at[slot_row].set(jnp.arange(tok_rows, dtype=jnp.int32))
    )
    arrived_hidden, arrived_grad = (
        lax.all_to_all(hidden_two[inverse_order], "dp", split_axis=0, concat_axis=0, tiled=True),
        lax.all_to_all(cotangent[inverse_order], "dp", split_axis=0, concat_axis=0, tiled=True),
    )
    members = arrived_hidden.reshape(data_ranks, groups_here, per_source, D)
    grad_update = arrived_grad.reshape(data_ranks, groups_here, per_source, D)
    logits = jnp.einsum("ngsd,de->ngse", members, router_weight, preferred_element_type=jnp.float32)
    exponent = jnp.exp(logits - jnp.max(logits, axis=(0, 2), keepdims=True))
    mixing = exponent / jnp.sum(exponent, axis=(0, 2), keepdims=True)
    mixing_low = mixing.astype(jnp.bfloat16)
    mixed_rows = jnp.einsum(
        "ngse,ngsd->egd", mixing_low, members, preferred_element_type=jnp.float32
    ).astype(jnp.bfloat16)
    expert_rows = lax.all_to_all(mixed_rows, "tensor", split_axis=0, concat_axis=0, tiled=True)
    expert_rows = expert_rows.reshape(tensor_size, experts_here, groups_here, D)
    pre_act = jnp.einsum(
        "tegd,edf->tegf", expert_rows, expert_in, preferred_element_type=jnp.float32
    )
    activated = jax.nn.gelu(pre_act, approximate=True).astype(jnp.bfloat16)
    produced = jnp.einsum(
        "tegf,efd->tegd", activated, expert_out, preferred_element_type=jnp.float32
    ).astype(jnp.bfloat16)
    returned = lax.all_to_all(
        produced.reshape(experts_all, groups_here, D),
        "tensor",
        split_axis=0,
        concat_axis=0,
        tiled=True,
    )
    spread = jnp.einsum("ngse,egd->ngsd", mixing_low, returned, preferred_element_type=jnp.float32)
    back_rows = lax.all_to_all(
        spread.reshape(tok_rows, D).astype(jnp.bfloat16),
        "dp",
        split_axis=0,
        concat_axis=0,
        tiled=True,
    )
    block_out = (residual_one + back_rows[slot_row].astype(jnp.float32)).astype(jnp.bfloat16)
    grad_produced = jnp.einsum(
        "ngse,ngsd->egd", mixing_low, grad_update, preferred_element_type=jnp.float32
    ).astype(jnp.bfloat16)
    grad_mixing = jnp.einsum(
        "ngsd,egd->ngse", grad_update, returned, preferred_element_type=jnp.float32
    )
    expert_grads = lax.all_to_all(grad_produced, "tensor", split_axis=0, concat_axis=0, tiled=True)
    expert_grads = expert_grads.reshape(tensor_size, experts_here, groups_here, D)
    grad_act = jnp.einsum(
        "tegd,efd->tegf", expert_grads, expert_out, preferred_element_type=jnp.float32
    )
    gelu_value, gelu_back = jax.vjp(partial(jax.nn.gelu, approximate=True), pre_act)
    grad_pre = gelu_back(grad_act)[0].astype(jnp.bfloat16)
    grad_mixed = jnp.einsum(
        "tegf,edf->tegd", grad_pre, expert_in, preferred_element_type=jnp.float32
    ).astype(jnp.bfloat16)
    local_in = jnp.einsum(
        "tegd,tegf->edf", expert_rows, grad_pre, preferred_element_type=jnp.float32
    )
    local_out = jnp.einsum(
        "tegf,tegd->efd", activated, expert_grads, preferred_element_type=jnp.float32
    )
    grad_mixed_all = lax.all_to_all(
        grad_mixed.reshape(experts_all, groups_here, D),
        "tensor",
        split_axis=0,
        concat_axis=0,
        tiled=True,
    )
    grad_mixing = grad_mixing + jnp.einsum(
        "egd,ngsd->ngse", grad_mixed_all, members, preferred_element_type=jnp.float32
    )
    grad_member = jnp.einsum(
        "ngse,egd->ngsd", mixing_low, grad_mixed_all, preferred_element_type=jnp.float32
    )
    inner_sum = jnp.sum(mixing * grad_mixing, axis=(0, 2), keepdims=True)
    grad_logits = (mixing * (grad_mixing - inner_sum)).astype(jnp.bfloat16)
    router_part = jnp.einsum(
        "ngsd,ngse->de", members, grad_logits, preferred_element_type=jnp.float32
    )
    grad_member = grad_member + jnp.einsum(
        "ngse,de->ngsd", grad_logits, router_weight, preferred_element_type=jnp.float32
    )
    grad_sorted = lax.all_to_all(
        grad_member.reshape(tok_rows, D).astype(jnp.bfloat16),
        "dp",
        split_axis=0,
        concat_axis=0,
        tiled=True,
    )
    grad_hidden_two = grad_sorted[slot_row].astype(jnp.float32)
    gain_two_part = jnp.sum(grad_hidden_two * normed_two, axis=0)
    grad_residual = cotangent.astype(jnp.float32) + norm_back(
        grad_hidden_two, normed_two, scale_two, norm2_gain
    )
    grad_rows = lax.all_gather(grad_residual.astype(jnp.bfloat16), "tensor", axis=0, tiled=True)
    grad_attn_out = lax.dot_general(
        attn_low, grad_rows, contract_first, preferred_element_type=jnp.float32
    )
    grad_attended = lax.dot_general(
        grad_rows, out_weight, contract_last, preferred_element_type=jnp.float32
    )
    grad_attended = grad_attended.astype(jnp.bfloat16).reshape(length_all, local_heads, head_size)

    def back_block(running, block_pair):
        offset, block_totals = block_pair
        grad_keys, grad_values = running
        query_rows = lax.dynamic_slice_in_dim(queries, offset, block_rows, 0)
        grad_rows_out = lax.dynamic_slice_in_dim(grad_attended, offset, block_rows, 0)
        scores = block_scores(query_rows, all_keys, offset, block_rows, doc_ids, places, factor)
        weights = jnp.exp(scores - block_totals[:, :, None])
        grad_values = grad_values + jnp.einsum(
            "hqk,qhd->khd",
            weights.astype(jnp.bfloat16),
            grad_rows_out,
            preferred_element_type=jnp.float32,
        )
        grad_weights = jnp.einsum(
            "qhd,khd->hqk", grad_rows_out, all_values, preferred_element_type=jnp.float32
        )
        row_inner = jnp.sum(weights * grad_weights, axis=-1, keepdims=True)
        grad_scores = (weights * (grad_weights - row_inner) * factor).astype(jnp.bfloat16)
        grad_query = jnp.einsum(
            "hqk,khd->qhd", grad_scores, all_keys, preferred_element_type=jnp.float32
        )
        grad_keys = grad_keys + jnp.einsum(
            "hqk,qhd->khd", grad_scores, query_rows, preferred_element_type=jnp.float32
        )
        return ((grad_keys, grad_values), grad_query)

    empty_heads = jnp.zeros((length_all, local_heads, head_size), jnp.float32)
    (grad_keys, grad_values), grad_queries = lax.scan(
        back_block, (empty_heads, empty_heads), (offsets, log_totals)
    )
    grad_queries = grad_queries.reshape(length_all, local_heads, head_size)
    grad_projected = jnp.stack((grad_queries, grad_keys, grad_values), axis=2)
    grad_projected = grad_projected.reshape(length_all, 3 * local_heads * head_size).astype(
        jnp.bfloat16
    )
    grad_qkv_part = lax.dot_general(
        rows_one, grad_projected, contract_first, preferred_element_type=jnp.float32
    )
    grad_hidden_one = lax.psum_scatter(
        lax.dot_general(
            grad_projected, qkv_weight, contract_last, preferred_element_type=jnp.float32
        ).astype(jnp.bfloat16),
        "tensor",
        scatter_dimension=0,
        tiled=True,
    ).astype(jnp.float32)
    gain_one_part = jnp.sum(grad_hidden_one * normed_one, axis=0)
    grad_tokens = (
        grad_residual + norm_back(grad_hidden_one, normed_one, scale_one, norm1_gain)
    ).astype(jnp.bfloat16)
    grad_norm1, grad_norm2, grad_router = lax.psum(
        (gain_one_part, gain_two_part, router_part), ("dp", "tensor")
    )
    weight_terms = (grad_qkv_part, grad_attn_out, local_in, local_out)
    summed = (
        lax.psum(weight_terms[0].astype(jnp.bfloat16), "dp").astype(jnp.float32),
        lax.psum(weight_terms[1].astype(jnp.bfloat16), "dp").astype(jnp.float32),
        lax.psum(weight_terms[2].astype(jnp.bfloat16), "dp").astype(jnp.float32),
        lax.psum(weight_terms[3].astype(jnp.bfloat16), "dp").astype(jnp.float32),
    )
    final_in, final_out = (summed[2], summed[3])
    return (
        block_out,
        grad_tokens,
        grad_norm1,
        summed[0],
        summed[1],
        grad_norm2,
        grad_router,
        final_in,
        final_out,
    )


def solution(mesh):
    in_specs = (
        P(("dp", "tensor"), None),
        P(("dp", "tensor"), None),
        P("dp", None),
        P(("dp", "tensor"), None),
        P(),
        P(None, "tensor"),
        P("tensor", None),
        P(),
        P(),
        P("tensor", None, None),
        P("tensor", None, None),
    )
    out_specs = (
        P(("dp", "tensor"), None),
        P(("dp", "tensor"), None),
        P(),
        P(None, "tensor"),
        P("tensor", None),
        P(),
        P(),
        P("tensor", None, None),
        P("tensor", None, None),
    )
    return jax.shard_map(local, mesh=mesh, in_specs=in_specs, out_specs=out_specs, check_vma=False)
```

profile of v0, /device:TPU:0, one launch (start us, length us, event | category | flops | bytes accessed | tf_op | source)
XLA Modules:
  0.0 989.5 jit_solution(15148079393786577822)
XLA Ops:
  11.6 30.6 %all-gather.3.cloned.1.call-done = bf16[2048,512]{1,0:T(8,128)(2,1)} async-done(((bf16[512,512]{1,0:T(8,128)(2,1)}), bf16[2048,512]{1,0:T(8,128)(2,1)}) %all-gather.3.cloned.1.call-update) | async-done | bytes 2097168 | tf_op jit(solution)/shard_map/all_gather | solution.py:70
  45.9 50.7 %while.29 = (s32[]{:T(128)}, bf16[4,512,2,64]{1,3,2,0:T(8,128)(2,1)S(1)}, f32[4,2,512]{2,1,0:T(2,128)}, s32[4]{0:T(128)S(1)}, s32[2048]{0:T(1024)S(1)}, /*index=...) while((s32[]{:T(128)}, ...), condition=%wide.region_6.7_spmd.clone, body=%wide.region_3.6_spmd.clone.sunk | while | flops 565181440 | bytes 30863552 | solution.py:94
  102.6 26.9 %reduce-scatter.3.cloned.1.call-done = bf16[512,512]{1,0:T(8,128)(2,1)} async-done(((bf16[2048,512]{1,0:T(8,128)(2,1)}), bf16[512,512]{1,0:T(8,128)(2,1)}) %reduce-scatter.3.cloned.1.call-update) | async-done | bytes 524304 | tf_op jit(solution)/shard_map/reduce_scatter | solution.py:96
  134.7 9.4 all-to-all-start
  146.7 11.4 %all-to-all-done = bf16[32,16,512]{2,1,0:T(8,128)(2,1)S(1)} async-done(((bf16[32,16,512]{2,1,0:T(8,128)(2,1)}), bf16[32,16,512]{2,1,0:T(8,128)(2,1)S(1)}, u32[]{:S(2)}, u32[]{:S(2)}) %all-to-all-start) | async-done | bytes 524320 | tf_op jit(solution)/shard_map/all_to_all | solution.py:110
  165.0 10.1 %all-to-all-done.4 = bf16[32,16,512]{2,1,0:T(8,128)(2,1)S(1)} async-done(((bf16[32,16,512]{2,1,0:T(8,128)(2,1)}), bf16[32,16,512]{2,1,0:T(8,128)(2,1)S(1)}, u32[]{:S(2)}, u32[]{:S(2)}) %all-to-all-start.4) | async-done | bytes 524320 | tf_op jit(solution)/shard_map/all_to_all | solution.py:111
  225.7 13.0 %all-to-all-done.7 = bf16[32,16,512]{2,1,0:T(8,128)(2,1)S(1)} async-done(((bf16[32,16,512]{2,1,0:T(8,128)(2,1)}), bf16[32,16,512]{2,1,0:T(8,128)(2,1)S(1)}, u32[]{:S(2)}, u32[]{:S(2)}) %all-to-all-start.7) | async-done | bytes 524320 | tf_op jit(solution)/shard_map/all_to_all | solution.py:190
  245.1 24.3 %all-gather.5.cloned.1.call-done = bf16[2048,512]{1,0:T(8,128)(2,1)} async-done(((bf16[512,512]{1,0:T(8,128)(2,1)}), bf16[2048,512]{1,0:T(8,128)(2,1)}) %all-gather.5.cloned.1.call-update) | async-done | bytes 2097168 | tf_op jit(solution)/shard_map/all_gather | solution.py:202
  273.5 216.9 %while.30 = (s32[]{:T(128)}, f32[2048,2,64]{0,2,1:T(8,128)}, f32[2048,2,64]{0,2,1:T(8,128)}, bf16[4,512,2,64]{1,3,2,0:T(8,128)(2,1)}, s32[4]{0:T(128)}, /*index=...) while((s32[]{:T(128)}, f32[2048,2,64]{0,2,1:T(8,128)}, ...), condition=%wide.region_16.17_spmd.clone.clone, body=%wide.region_14.16_spmd.clone.clone.sunk | while | flops 1400903680 | bytes 149234032 | solution.py:238
  288.5 4.8 fusion.229
  293.3 16.5 %fusion.233 = bf16[4,512,2,64]{1,3,2,0:T(8,128)(2,1)} fusion(bf16[4,512,2,64]{1,3,2,0:T(8,128)(2,1)} %get-tuple-element.471, s32[]{:T(128)S(6)} %copy.204, bf16[2048,2,64]{0,2,1:T(8,128)(2,1)} %get-tuple-element.491, f32[2,512,2048]{2,1,0:T(8,128)} %fusion.229, f32[2,512,2048]{2,1,0:T(8,128)} %copy-done.1, f32[2,512]{1,0:T(2,128)} %copy-done.28, ...), kind=kOutput, calls=%fused_computation.44.clone.1 | convolution fusion | flops 291507200 | bytes 36446212 | tf_op jit(solution)/shard_map/while/body/eval_jaxpr/hqk,khd->qhd/dot_general | solution.py:229
  309.8 18.2 %fusion.231 = f32[2048,2,64]{0,2,1:T(8,128)} fusion(f32[2,512,2048]{2,1,0:T(8,128)} %fusion.229, f32[2,512,2048]{2,1,0:T(8,128)} %copy-done.1, f32[2,512]{1,0:T(2,128)} %copy-done.28, pred[512,2048]{1,0:T(8,128)(4,1)S(1)} %compare_and_fusion.5, f32[2048,2,64]{0,2,1:T(8,128)} %get-tuple-element.469, pred[]{:T(512)S(6)} %compare.3, ...), kind=kOutput, calls=%fused_computation.42.clone.1 | convolution fusion | flops 292031488 | bytes 37888004 | tf_op jit(solution)/shard_map/while/body/eval_jaxpr/hqk,qhd->khd/dot_general | solution.py:232
  347.4 16.5 %fusion.233 = bf16[4,512,2,64]{1,3,2,0:T(8,128)(2,1)} fusion(bf16[4,512,2,64]{1,3,2,0:T(8,128)(2,1)} %get-tuple-element.471, s32[]{:T(128)S(6)} %copy.204, bf16[2048,2,64]{0,2,1:T(8,128)(2,1)} %get-tuple-element.491, f32[2,512,2048]{2,1,0:T(8,128)} %fusion.229, f32[2,512,2048]{2,1,0:T(8,128)} %copy-done.1, f32[2,512]{1,0:T(2,128)} %copy-done.28, ...), kind=kOutput, calls=%fused_computation.44.clone.1 | convolution fusion | flops 291507200 | bytes 36446212 | tf_op jit(solution)/shard_map/while/body/eval_jaxpr/hqk,khd->qhd/dot_general | solution.py:229
  363.9 18.1 %fusion.231 = f32[2048,2,64]{0,2,1:T(8,128)} fusion(f32[2,512,2048]{2,1,0:T(8,128)} %fusion.229, f32[2,512,2048]{2,1,0:T(8,128)} %copy-done.1, f32[2,512]{1,0:T(2,128)} %copy-done.28, pred[512,2048]{1,0:T(8,128)(4,1)S(1)} %compare_and_fusion.5, f32[2048,2,64]{0,2,1:T(8,128)} %get-tuple-element.469, pred[]{:T(512)S(6)} %compare.3, ...), kind=kOutput, calls=%fused_computation.42.clone.1 | convolution fusion | flops 292031488 | bytes 37888004 | tf_op jit(solution)/shard_map/while/body/eval_jaxpr/hqk,qhd->khd/dot_general | solution.py:232
  396.7 4.8 fusion.229
  401.5 16.5 %fusion.233 = bf16[4,512,2,64]{1,3,2,0:T(8,128)(2,1)} fusion(bf16[4,512,2,64]{1,3,2,0:T(8,128)(2,1)} %get-tuple-element.471, s32[]{:T(128)S(6)} %copy.204, bf16[2048,2,64]{0,2,1:T(8,128)(2,1)} %get-tuple-element.491, f32[2,512,2048]{2,1,0:T(8,128)} %fusion.229, f32[2,512,2048]{2,1,0:T(8,128)} %copy-done.1, f32[2,512]{1,0:T(2,128)} %copy-done.28, ...), kind=kOutput, calls=%fused_computation.44.clone.1 | convolution fusion | flops 291507200 | bytes 36446212 | tf_op jit(solution)/shard_map/while/body/eval_jaxpr/hqk,khd->qhd/dot_general | solution.py:229
  418.0 18.2 %fusion.231 = f32[2048,2,64]{0,2,1:T(8,128)} fusion(f32[2,512,2048]{2,1,0:T(8,128)} %fusion.229, f32[2,512,2048]{2,1,0:T(8,128)} %copy-done.1, f32[2,512]{1,0:T(2,128)} %copy-done.28, pred[512,2048]{1,0:T(8,128)(4,1)S(1)} %compare_and_fusion.5, f32[2048,2,64]{0,2,1:T(8,128)} %get-tuple-element.469, pred[]{:T(512)S(6)} %compare.3, ...), kind=kOutput, calls=%fused_computation.42.clone.1 | convolution fusion | flops 292031488 | bytes 37888004 | tf_op jit(solution)/shard_map/while/body/eval_jaxpr/hqk,qhd->khd/dot_general | solution.py:232
  455.6 16.5 %fusion.233 = bf16[4,512,2,64]{1,3,2,0:T(8,128)(2,1)} fusion(bf16[4,512,2,64]{1,3,2,0:T(8,128)(2,1)} %get-tuple-element.471, s32[]{:T(128)S(6)} %copy.204, bf16[2048,2,64]{0,2,1:T(8,128)(2,1)} %get-tuple-element.491, f32[2,512,2048]{2,1,0:T(8,128)} %fusion.229, f32[2,512,2048]{2,1,0:T(8,128)} %copy-done.1, f32[2,512]{1,0:T(2,128)} %copy-done.28, ...), kind=kOutput, calls=%fused_computation.44.clone.1 | convolution fusion | flops 291507200 | bytes 36446212 | tf_op jit(solution)/shard_map/while/body/eval_jaxpr/hqk,khd->qhd/dot_general | solution.py:229
  472.1 18.1 %fusion.231 = f32[2048,2,64]{0,2,1:T(8,128)} fusion(f32[2,512,2048]{2,1,0:T(8,128)} %fusion.229, f32[2,512,2048]{2,1,0:T(8,128)} %copy-done.1, f32[2,512]{1,0:T(2,128)} %copy-done.28, pred[512,2048]{1,0:T(8,128)(4,1)S(1)} %compare_and_fusion.5, f32[2048,2,64]{0,2,1:T(8,128)} %get-tuple-element.469, pred[]{:T(512)S(6)} %compare.3, ...), kind=kOutput, calls=%fused_computation.42.clone.1 | convolution fusion | flops 292031488 | bytes 37888004 | tf_op jit(solution)/shard_map/while/body/eval_jaxpr/hqk,qhd->khd/dot_general | solution.py:232
  512.7 9.4 all-to-all-start.3
  523.2 15.4 %all-to-all-done.3 = bf16[32,16,512]{2,1,0:T(8,128)(2,1)S(1)} async-done(((bf16[32,16,512]{2,1,0:T(8,128)(2,1)}), bf16[32,16,512]{2,1,0:T(8,128)(2,1)S(1)}, u32[]{:S(2)}, u32[]{:S(2)}) %all-to-all-start.3) | async-done | bytes 524320 | tf_op jit(solution)/shard_map/all_to_all | solution.py:139
  542.3 386.6 %all-reduce = (f32[512]{0:T(512)}, f32[512]{0:T(512)}, f32[512,8]{0,1:T(8,128)}) all-reduce(f32[512]{0:T(512)S(1)} %get-tuple-element.223, f32[512]{0:T(512)} %get-tuple-element.221, f32[512,8]{0,1:T(8,128)S(1)} %convolution_bitcast_fusion.2), channel_id=1, replica_groups=mesh['dp'=32,'tensor'=4] {'dp','tensor'}, use_global_device_ids=true, to_apply=%region_20.21 | all-reduce | flops 5120 | bytes 40960 | tf_op jit(solution)/shard_map/psum | solution.py:261
  931.7 36.0 %all-reduce.4.cloned.1.call-done = (bf16[512,384]{1,0:T(8,128)(2,1)}, bf16[128,512]{1,0:T(8,128)(2,1)}, bf16[2,512,2048]{2,1,0:T(8,128)(2,1)}, bf16[2,2048,512]{2,1,0:T(8,128)(2,1)}) async-done(((bf16[512,384]{1,0:T(8,128)(2,1)}, bf16[128,512]{1,0:T(8,128)(2,1)}, bf16[2,512,2048]{2,1,0:T(8,128)(2,1)}, bf16[2,2048,512]{2,1,0:T(8,128)(2,1)}), (bf16[512,384]{1,0:T(8,128)(2,1)}, bf16[128,512]{1,0:T(8,128)(2,1)}, ...) | async-done | bytes 8912912 | tf_op jit(solution)/shard_map/psum | solution.py:266
  971.5 6.7 convert_element_type.190
  (269 shorter events, 230.5 us)
Async XLA Ops:
  7.2 35.0 %all-gather.3.cloned.1.call-start = ((), (), s32[]{:S(2)}) async-start(), calls=%async_computation.10 | async-start | bytes 2621440 | tf_op jit(solution)/shard_map/all_gather | solution.py:70
  8.5 37.4 %copy-start.30 = (f32[512]{0:T(512)}, f32[512]{0:T(512)S(1)}, u32[]{:S(2)}) copy-start(f32[512]{0:T(512)S(1)} %add_rsqrt_fusion.1) | copy-start | bytes 6148
  10.6 118.9 %reduce-scatter.3.cloned.1.call-start = ((), (), s32[]{:S(2)}) async-start(), calls=%async_computation.11 | async-start | bytes 2621440 | tf_op jit(solution)/shard_map/reduce_scatter | solution.py:96
  45.9 52.1 %copy-start.25 = (bf16[128,512]{1,0:T(8,128)(2,1)S(1)}, bf16[128,512]{1,0:T(8,128)(2,1)}, u32[]{:S(2)}) copy-start(bf16[128,512]{1,0:T(8,128)(2,1)} %param.21) | copy-start | bytes 393220
  45.9 54.2 %copy-start.36 = (s32[1,512]{1,0:T(1,128)S(1)}, s32[1,512]{1,0:T(1,128)}, u32[]{:S(2)}) copy-start(s32[1,512]{1,0:T(1,128)} %param.18) | copy-start | bytes 6148
  45.9 83.6 %copy-start.3 = (bf16[512,512]{1,0:T(8,128)(2,1)S(1)}, bf16[512,512]{1,0:T(8,128)(2,1)}, u32[]{:S(2)}) copy-start(bf16[512,512]{1,0:T(8,128)(2,1)} %param.15) | copy-start | bytes 1572868
  45.9 84.9 %copy-start.31 = (f32[512]{0:T(512)S(1)}, f32[512]{0:T(512)}, u32[]{:S(2)}) copy-start(f32[512]{0:T(512)} %param.22) | copy-start | bytes 6148
  96.7 47.4 %copy-start.2 = (bf16[512,512]{1,0:T(8,128)(2,1)S(1)}, bf16[512,512]{1,0:T(8,128)(2,1)}, u32[]{:S(2)}) copy-start(bf16[512,512]{1,0:T(8,128)(2,1)} %param.16) | copy-start | bytes 1572868
  100.1 62.2 %copy-start.32 = (bf16[512,8]{0,1:T(8,128)(2,1)S(1)}, bf16[512,8]{0,1:T(8,128)(2,1)}, u32[]{:S(2)}) copy-start(bf16[512,8]{0,1:T(8,128)(2,1)} %param.23) | copy-start | bytes 24580
  100.1 58.0 %copy-start.35 = (s32[512,1]{0,1:T(1,128)}, s32[512,1]{0,1:T(1,128)S(1)}, u32[]{:S(2)}) copy-start(s32[512,1]{0,1:T(1,128)S(1)} %compare_select_fusion) | copy-start | bytes 6148
  134.7 23.4 %all-to-all-start = ((bf16[32,16,512]{2,1,0:T(8,128)(2,1)}), bf16[32,16,512]{2,1,0:T(8,128)(2,1)S(1)}, u32[]{:S(2)}, u32[]{:S(2)}) async-start(bf16[32,16,512]{2,1,0:T(8,128)(2,1)} %bitcast.8), calls=%async_computation.1 | async-start | bytes 1048576 | tf_op jit(solution)/shard_map/all_to_all | solution.py:110
  158.2 16.9 %all-to-all-start.4 = ((bf16[32,16,512]{2,1,0:T(8,128)(2,1)}), bf16[32,16,512]{2,1,0:T(8,128)(2,1)S(1)}, u32[]{:S(2)}, u32[]{:S(2)}) async-start(bf16[32,16,512]{2,1,0:T(8,128)(2,1)} %bitcast.23), calls=%async_computation.5 | async-start | bytes 1048576 | tf_op jit(solution)/shard_map/all_to_all | solution.py:111
  175.1 7.9 all-to-all-start.1
  183.0 10.5 %all-to-all-start.5 = ((bf16[8,16,512]{2,1,0:T(8,128)(2,1)}), bf16[8,16,512]{2,1,0:T(8,128)(2,1)S(1)}, u32[]{:S(2)}, u32[]{:S(2)}) async-start(bf16[8,16,512]{2,1,0:T(8,128)(2,1)} %copy.138), calls=%async_computation.6 | async-start | bytes 262144 | tf_op jit(solution)/shard_map/all_to_all | solution.py:153
  193.5 12.7 %all-to-all-start.2 = ((bf16[8,16,512]{2,1,0:T(8,128)(2,1)}), bf16[8,16,512]{2,1,0:T(8,128)(2,1)}, u32[]{:S(2)}, u32[]{:S(2)}) async-start(bf16[8,16,512]{2,1,0:T(8,128)(2,1)} %bitcast.18), calls=%async_computation.3 | async-start | bytes 262144 | tf_op jit(solution)/shard_map/all_to_all | solution.py:131
  201.9 38.7 %copy-start.4 = (bf16[512,512]{1,0:T(8,128)(2,1)S(1)}, bf16[512,512]{1,0:T(8,128)(2,1)}, u32[]{:S(2)}) copy-start(bf16[512,512]{1,0:T(8,128)(2,1)} %reduce-scatter.3.cloned.1.call-done) | copy-start | bytes 1572868
  206.3 7.9 all-to-all-start.6
  221.1 17.6 %all-to-all-start.7 = ((bf16[32,16,512]{2,1,0:T(8,128)(2,1)}), bf16[32,16,512]{2,1,0:T(8,128)(2,1)S(1)}, u32[]{:S(2)}, u32[]{:S(2)}) async-start(bf16[32,16,512]{2,1,0:T(8,128)(2,1)} %copy.150), calls=%async_computation.8 | async-start | bytes 1048576 | tf_op jit(solution)/shard_map/all_to_all | solution.py:190
  225.0 44.4 %all-gather.5.cloned.1.call-start = ((), (), s32[]{:S(2)}) async-start(), calls=%async_computation.12 | async-start | bytes 2621440 | tf_op jit(solution)/shard_map/all_gather | solution.py:202
  225.7 43.7 %copy-start.34 = (s32[1024]{0:T(1024)}, s32[1024]{0:T(1024)S(1)}, u32[]{:S(2)}) copy-start(s32[1024]{0:T(1024)S(1)} %pad_clamp_fusion) | copy-start | bytes 12292
  245.0 295.7 %reduce-scatter.5.cloned.1.call-start = ((), (), s32[]{:S(2)}) async-start(), calls=%async_computation.13 | async-start | bytes 2621440 | tf_op jit(solution)/shard_map/reduce_scatter | solution.py:249
  498.2 469.5 %all-reduce.4.cloned.1.call-start = ((), (), s32[]{:S(2)}) async-start(), calls=%async_computation.14 | async-start | bytes 17825792 | tf_op jit(solution)/shard_map/psum | solution.py:266
  510.3 418.6 %copy-start.8 = (bf16[512,512]{1,0:T(8,128)(2,1)S(1)}, bf16[512,512]{1,0:T(8,128)(2,1)}, u32[]{:S(2)}) copy-start(bf16[512,512]{1,0:T(8,128)(2,1)} %copy-done.7) | copy-start | bytes 1572868
  512.7 25.9 %all-to-all-start.3 = ((bf16[32,16,512]{2,1,0:T(8,128)(2,1)}), bf16[32,16,512]{2,1,0:T(8,128)(2,1)S(1)}, u32[]{:S(2)}, u32[]{:S(2)}) async-start(bf16[32,16,512]{2,1,0:T(8,128)(2,1)} %copy.135), calls=%async_computation.4 | async-start | bytes 1048576 | tf_op jit(solution)/shard_map/all_to_all | solution.py:139
  (43 other events, 369.4 us)
Sparse Core Ops, SparseCore 0:
  10.7 31.4 all-gather.2
  100.2 29.2 reduce-scatter.2
  245.1 24.2 all-gather.4
  498.3 32.1 reduce-scatter.4
  534.2 433.4 all-reduce.3
where the time goes:
time: 1000 us; the launch traced here: 989 us
  blocking collectives  387 us (39%)
  matrix products  248 us (25%)
  waiting for transfers between devices  174 us (17%)
  local copies, waits for them, and re-layouts  54.7 us (5%)
  other arithmetic  54.2 us (5%)
  starting transfers between devices  40.9 us (4%)
  loops' own time  16.4 us (2%)
  between operations  14.6 us (1%)
    psum x1, blocking collectives, local(): lax.psum((gain_one_part, gain_two_part, router_part), ('dp', 'tensor'))  387 us
    dot_general x4, matrix products, back_block(): jnp.einsum('hqk,qhd->khd', grad_scores, query_rows, preferred_element_typ...  72.7 us
    dot_general x4, matrix products, back_block(): jnp.einsum('hqk,khd->qhd', grad_scores, all_keys, preferred_element_type=...  65.9 us
    psum x1, waiting for transfers between devices, local(): lax.psum(weight_terms[0].astype(jnp.bfloat16), 'dp').astype(jnp.float32)  36 us
    all_gather x1, waiting for transfers between devices, local(): rows_one = lax.all_gather(hidden_one, 'tensor', axis=0, tiled=True)  30.6 us
    reduce_scatter x1, waiting for transfers between devices, local(): lax.psum_scatter(jnp.dot(attn_low, out_weight, preferred_element_type=jnp...  26.9 us
    all_gather x1, waiting for transfers between devices, local(): lax.all_gather(grad_residual.astype(jnp.bfloat16), 'tensor', axis=0, tile...  24.3 us
    dot_general x8, matrix products, block_scores(): jnp.einsum('qhd,khd->hqk', query_rows, all_keys, preferred_element_type=j...  23.2 us
  transfers between devices with their start and end apart: 13, of which 10 were waited for; matrix products, arithmetic and copies ran while one was open for 5% of the time, Pallas kernels for 0%

commit v1 on v0

v1 whole, which is shorter than its diff:
```python
from functools import partial

import jax
import jax.numpy as jnp
from jax import lax
from jax.experimental import pallas as pl
from jax.experimental.pallas import tpu as pltpu
from jax.sharding import PartitionSpec as P

D = 512
GROUP = 32
ROWS = 512
LENGTH = 2048
N_DP = 32
PER = ROWS // N_DP
CHUNKS = 4
MESH = pl.DeviceIdType.MESH
NN = (((1,), (0,)), ((), ()))
NT = (((1,), (1,)), ((), ()))
TN = (((0,), (0,)), ((), ()))
f32 = jnp.float32
bf16 = jnp.bfloat16
eps = 1e-06


def dot(a, b, dims=NN):
    return lax.dot_general(a, b, dims, preferred_element_type=f32)


def normalize(values):
    factor = lax.rsqrt(jnp.mean(values * values, axis=-1, keepdims=True) + eps)
    return (values * factor, factor)


def norm_back(grad_hidden, normed, factor, gain_row):
    grad_normed = grad_hidden * gain_row
    inner_sum = jnp.mean(grad_normed * normed, axis=-1, keepdims=True)
    return factor * (grad_normed - normed * inner_sum)


def remote(src, dst, send_sem, recv_sem, device):
    return pltpu.make_async_remote_copy(
        src_ref=src,
        dst_ref=dst,
        send_sem=send_sem,
        recv_sem=recv_sem,
        device_id=device,
        device_id_type=MESH,
    )


def document_starts(lengths, base, count):
    place = lax.broadcasted_iota(jnp.int32, (1, count), 1) + base
    bound = jnp.int32(0)
    first = jnp.zeros((1, count), jnp.int32)
    for slot in range(9):
        bound = bound + lengths[0, slot]
        first = jnp.where(bound <= place, bound, first)
    return place, first


def allowed_pairs(place, first, key_base, keys):
    key = lax.broadcasted_iota(jnp.int32, (keys, place.shape[1]), 0)
    return (key >= first - key_base) & (key <= place - key_base)


def attend_block(lengths, q2, k, v2t, base, rows):
    place, first = document_starts(lengths, base, rows)

    def step(index, carry):
        key_base = pl.multiple_of(index * rows, rows)
        allowed = allowed_pairs(place, first, key_base, rows)
        keys = k[pl.ds(key_base, rows), :]
        result = []
        for head in range(2):
            scores = jnp.where(allowed, dot(keys, q2[head, pl.ds(base, rows), :], NT), -1e30)
            maxima = jnp.max(scores, axis=0, keepdims=True)
            if carry is not None:
                maxima = jnp.maximum(carry[head][0], maxima)
            weights = jnp.exp(scores - maxima).astype(bf16)
            total = dot(v2t[head, :, pl.ds(key_base, rows)], weights)
            if carry is not None:
                total = carry[head][1] * jnp.exp(carry[head][0] - maxima) + total
            result.append((maxima, total))
        return tuple(result)

    blocks = base // rows
    carry = step(blocks, None)
    if blocks > 0:
        carry = lax.fori_loop(0, blocks, lambda i, c: step(blocks - 1 - i, c), carry)
    (max_a, sum_a), (max_b, sum_b) = carry
    norm_a, norm_b = sum_a[64:65], sum_b[0:1]
    attended = jnp.concatenate([sum_a[:64] / norm_a, sum_b[64:] / norm_b], axis=0)
    return attended.T.astype(bf16), max_a + jnp.log(norm_a), max_b + jnp.log(norm_b)


def dp_exchange_start(source, target, send_sems, recv_sems):
    me, t = lax.axis_index("dp"), lax.axis_index("tensor")
    mine = pl.ds(pl.multiple_of(me * PER, PER), PER)

    def send(k, carry):
        peer = (me + k) % N_DP
        remote(
            source.at[pl.ds(pl.multiple_of(peer * PER, PER), PER)],
            target.at[mine],
            send_sems.at[k],
            recv_sems.at[k],
            (peer, t),
        ).start()
        return carry

    lax.fori_loop(1, N_DP, send, 0)
    target[mine] = source[mine]


def dp_exchange_wait(source, target, send_sems, recv_sems):
    me, t = lax.axis_index("dp"), lax.axis_index("tensor")

    def wait(k, carry):
        sent = (me + k) % N_DP
        came = (me + N_DP - k) % N_DP
        remote(
            source.at[pl.ds(pl.multiple_of(sent * PER, PER), PER)],
            target.at[pl.ds(pl.multiple_of(came * PER, PER), PER)],
            send_sems.at[k],
            recv_sems.at[k],
            (sent, t),
        ).wait()
        return carry

    lax.fori_loop(1, N_DP, wait, 0)


def front_kernel(
    lengths,
    tokens,
    cotangent,
    slot,
    gain_one,
    qkv,
    out_w,
    gain_two,
    members,
    grad_update,
    residual,
    hidden,
    q2,
    k,
    v,
    k2t,
    lse,
    att_own,
    att_pos,
    out_all,
    perm,
    sorted_grad,
    sorted_hidden,
    v2t,
    hid_s,
    hid_r,
    out_s,
    out_r,
    att_s,
    att_r,
    grad_s,
    grad_r,
    mem_s,
    mem_r,
):
    me, t = lax.axis_index("dp"), lax.axis_index("tensor")
    sibling, cross, far = t + 1 - 2 * (t % 2), (t + 2) % 4, 3 - t
    barrier = pltpu.get_barrier_semaphore()
    for peer in (sibling, cross, far):
        pl.semaphore_signal(barrier, inc=1, device_id=(me, peer), device_id_type=MESH)

    def greet(i, carry):
        pl.semaphore_signal(barrier, inc=1, device_id=((me + i) % N_DP, t), device_id_type=MESH)
        return carry

    lax.fori_loop(1, N_DP, greet, 0)

    step = ROWS // CHUNKS
    for c in range(CHUNKS):
        values = tokens[c * step : (c + 1) * step, :].astype(f32)
        normed, _ = normalize(values)
        hidden[pl.ds(pl.multiple_of(t * ROWS + c * step, step), step), :] = (
            normed * gain_one[...]
        ).astype(bf16)
    out_all[t] = out_w[...]
    pl.semaphore_wait(barrier, N_DP + 2)

    def hidden_copy(kind, owner, c, device):
        rows = pl.ds(pl.multiple_of(owner * ROWS + c * step, step), step)
        return remote(
            hidden.at[rows], hidden.at[rows], hid_s.at[kind, c], hid_r.at[kind, c], (me, device)
        )

    for c in range(CHUNKS):
        hidden_copy(1, t, c, cross).start()
        hidden_copy(0, t, c, sibling).start()

    place = lax.broadcasted_iota(jnp.int32, (ROWS, ROWS), 0)
    perm[...] = jnp.where(place == slot[...], 1.0, 0.0).astype(bf16)
    sorted_grad[...] = dot(perm[...], cotangent[...]).astype(bf16)

    lane = lax.broadcasted_iota(jnp.int32, (D, 128), 1)
    part_a, part_b, part_c = (qkv[:, 128 * i : 128 * (i + 1)].astype(f32) for i in range(3))
    wq = jnp.where(lane < 64, part_a, part_b).astype(bf16)
    wk = pltpu.roll(jnp.where(lane < 64, part_c, part_a), 64, 1).astype(bf16)
    wv = jnp.where(lane < 64, part_b, part_c).astype(bf16)

    half = lax.broadcasted_iota(jnp.int32, (ROWS, 128), 1) < 64
    half_t = lax.broadcasted_iota(jnp.int32, (128, ROWS), 0) < 64

    def project(owner):
        rows = pl.ds(pl.multiple_of(owner * ROWS, ROWS), ROWS)
        block = hidden[rows, :]
        queries = dot(block, wq).astype(bf16).astype(f32) * 0.125
        q2[0, rows, :] = jnp.where(half, queries, 0.0).astype(bf16)
        q2[1, rows, :] = jnp.where(half, 0.0, queries).astype(bf16)
        keys = dot(block, wk)
        k[rows, :] = keys.astype(bf16)
        keys_t = keys.T
        k2t[0, :, rows] = jnp.where(half_t, keys_t, 0.0).astype(bf16)
        k2t[1, :, rows] = jnp.where(half_t, 0.0, keys_t).astype(bf16)
        values = dot(block, wv)
        v[rows, :] = values.astype(bf16)
        values_t = values.T
        v2t[0, :, rows] = jnp.where(half_t, values_t, 1.0).astype(bf16)
        v2t[1, :, rows] = jnp.where(half_t, 1.0, values_t).astype(bf16)

    project(t)
    for c in range(CHUNKS):
        hidden_copy(0, sibling, c, sibling).wait_recv()
    project(sibling)
    for c in range(CHUNKS):
        hidden_copy(1, cross, c, cross).wait_recv()
        hidden_copy(2, cross, c, sibling).start()
    project(cross)
    for c in range(CHUNKS):
        hidden_copy(2, far, c, sibling).wait_recv()
    project(far)

    def out_copy(i, device):
        return remote(out_all.at[t], out_all.at[t], out_s.at[i], out_r.at[i], (me, device))

    for i, peer in enumerate((sibling, cross, far)):
        out_copy(i, peer).start()
    dp_exchange_start(sorted_grad, grad_update, grad_s, grad_r)

    def att_copy(block, device):
        return remote(
            att_own.at[pl.ds(block * ROWS, ROWS)],
            att_pos.at[t],
            att_s.at[block],
            att_r.at[t],
            (me, device),
        )

    for block in range(4):
        rows = pl.ds(block * ROWS, ROWS)
        attended, lse_a, lse_b = attend_block(lengths, q2, k, v2t, block * ROWS, ROWS)
        att_own[rows, :] = attended
        lse[0:1, rows] = lse_a
        lse[1:2, rows] = lse_b

        @pl.when(t == block)
        def _():
            att_pos[t] = att_own[rows, :]

        @pl.when(t != block)
        def _():
            att_copy(block, block).start()

    for i, peer in enumerate((sibling, cross, far)):
        out_copy(i, peer).wait()
    for block in range(4):

        @pl.when(t != block)
        def _():
            att_copy(block, block).wait_send()

    for peer in (sibling, cross, far):
        remote(
            att_own.at[pl.ds(0, ROWS)], att_pos.at[peer], att_s.at[0], att_r.at[peer], (me, peer)
        ).wait_recv()

    update = dot(att_pos[0], out_all[0])
    for i in range(1, 4):
        update = update + dot(att_pos[i], out_all[i])
    residual[...] = tokens[...].astype(f32) + update
    normed_two, _ = normalize(residual[...])
    hidden_two = (normed_two * gain_two[...]).astype(bf16)
    sorted_hidden[...] = dot(perm[...], hidden_two).astype(bf16)
    dp_exchange_start(sorted_hidden, members, mem_s, mem_r)

    for c in range(CHUNKS):
        hidden_copy(0, t, c, sibling).wait_send()
        hidden_copy(1, t, c, cross).wait_send()
        hidden_copy(2, cross, c, sibling).wait_send()
    dp_exchange_wait(sorted_grad, grad_update, grad_s, grad_r)
    dp_exchange_wait(sorted_hidden, members, mem_s, mem_r)


def front(lengths, tokens, cotangent, slot, gain_one, qkv, out_w, gain_two):
    sds = jax.ShapeDtypeStruct
    vmem = pl.BlockSpec(memory_space=pltpu.VMEM)
    dma = pltpu.SemaphoreType.DMA
    return pl.pallas_call(
        front_kernel,
        name="front",
        out_shape=(
            sds((ROWS, D), bf16),
            sds((ROWS, D), bf16),
            sds((ROWS, D), f32),
            sds((LENGTH, D), bf16),
            sds((2, LENGTH, 128), bf16),
            sds((LENGTH, 128), bf16),
            sds((LENGTH, 128), bf16),
            sds((2, 128, LENGTH), bf16),
            sds((2, LENGTH), f32),
            sds((LENGTH, 128), bf16),
            sds((4, ROWS, 128), bf16),
            sds((4, 128, D), bf16),
            sds((ROWS, ROWS), bf16),
        ),
        in_specs=[pl.BlockSpec(memory_space=pltpu.SMEM)] + [vmem] * 7,
        out_specs=[vmem] * 13,
        scratch_shapes=[
            pltpu.VMEM((ROWS, D), bf16),
            pltpu.VMEM((ROWS, D), bf16),
            pltpu.VMEM((2, 128, LENGTH), bf16),
            dma((3, CHUNKS)),
            dma((3, CHUNKS)),
            dma((3,)),
            dma((3,)),
            dma((4,)),
            dma((4,)),
            dma((N_DP,)),
            dma((N_DP,)),
            dma((N_DP,)),
            dma((N_DP,)),
        ],
        compiler_params=pltpu.CompilerParams(
            collective_id=0, has_side_effects=True, vmem_limit_bytes=56 * 2**20
        ),
    )(lengths, tokens, cotangent, slot, gain_one, qkv, out_w, gain_two)


def back_kernel(lengths, q2, k, k2t, v, do2, delta, lse, dq_t, dk, dv):
    rows = 512
    blocks = LENGTH // rows
    for block in reversed(range(blocks)):
        base = block * rows
        here = pl.ds(base, rows)
        place, first = document_starts(lengths, base, rows)

        def step(index, grad_q):
            key_base = pl.multiple_of(index * rows, rows)
            there = pl.ds(key_base, rows)
            allowed = allowed_pairs(place, first, key_base, rows)
            keys, values = k[there, :], v[there, :]
            grad_v, grad_k = None, None
            for head in range(2):
                queries, grads = q2[head, here, :], do2[head, here, :]
                scores = dot(keys, queries, NT)
                shifted = jnp.where(allowed, scores - lse[head : head + 1, here], -1e30)
                weights = jnp.exp(shifted)
                grad_w = dot(values, grads, NT)
                grad_s = (weights * (grad_w - delta[head : head + 1, here])).astype(bf16)
                part = dot(weights.astype(bf16), grads)
                grad_v = part if grad_v is None else grad_v + part
                part = dot(grad_s, queries)
                grad_k = part if grad_k is None else grad_k + part
                grad_q = grad_q + dot(k2t[head, :, there], grad_s)
            if block == blocks - 1:
                dk[there, :] = grad_k
                dv[there, :] = grad_v
            else:
                dk[there, :] += grad_k
                dv[there, :] += grad_v
            return grad_q

        grad_q = lax.fori_loop(0, block + 1, step, jnp.zeros((128, rows), f32))
        dq_t[:, here] = grad_q * 0.125


def back(*args):
    sds = jax.ShapeDtypeStruct
    vmem = pl.BlockSpec(memory_space=pltpu.VMEM)
    return pl.pallas_call(
        back_kernel,
        name="attention_back",
        out_shape=(sds((128, LENGTH), f32), sds((LENGTH, 128), f32), sds((LENGTH, 128), f32)),
        in_specs=[pl.BlockSpec(memory_space=pltpu.SMEM)] + [vmem] * 7,
        out_specs=[vmem] * 3,
        compiler_params=pltpu.CompilerParams(vmem_limit_bytes=56 * 2**20),
    )(*args)


def local(
    tokens,
    cotangent,
    doc_lengths,
    group_slot,
    norm1_gain,
    qkv_weight,
    out_weight,
    norm2_gain,
    router_weight,
    expert_in,
    expert_out,
):
    data_ranks = N_DP
    tensor_size = 4
    tok_rows = ROWS
    groups_here = PER
    per_source = 1
    experts_here = expert_in.shape[0]
    experts_all = router_weight.shape[1]
    contract_first = TN
    contract_last = NT
    (
        arrived_hidden,
        arrived_grad,
        residual_one,
        rows_one,
        q2,
        k,
        v,
        k2t,
        lse,
        att_own,
        att_pos,
        out_all,
        perm,
    ) = front(
        doc_lengths,
        tokens,
        cotangent,
        group_slot,
        norm1_gain[None],
        qkv_weight,
        out_weight,
        norm2_gain[None],
    )
    inputs = tokens.astype(f32)
    normed_one, scale_one = normalize(inputs)
    normed_two, scale_two = normalize(residual_one)
    slot_row = group_slot[0]
    members = arrived_hidden.reshape(data_ranks, groups_here, per_source, D)
    grad_update = arrived_grad.reshape(data_ranks, groups_here, per_source, D)
    logits = jnp.einsum("ngsd,de->ngse", members, router_weight, preferred_element_type=jnp.float32)
    exponent = jnp.exp(logits - jnp.max(logits, axis=(0, 2), keepdims=True))
    mixing = exponent / jnp.sum(exponent, axis=(0, 2), keepdims=True)
    mixing_low = mixing.astype(jnp.bfloat16)
    mixed_rows = jnp.einsum(
        "ngse,ngsd->egd", mixing_low, members, preferred_element_type=jnp.float32
    ).astype(jnp.bfloat16)
    expert_rows = lax.all_to_all(mixed_rows, "tensor", split_axis=0, concat_axis=0, tiled=True)
    expert_rows = expert_rows.reshape(tensor_size, experts_here, groups_here, D)
    pre_act = jnp.einsum(
        "tegd,edf->tegf", expert_rows, expert_in, preferred_element_type=jnp.float32
    )
    activated = jax.nn.gelu(pre_act, approximate=True).astype(jnp.bfloat16)
    produced = jnp.einsum(
        "tegf,efd->tegd", activated, expert_out, preferred_element_type=jnp.float32
    ).astype(jnp.bfloat16)
    returned = lax.all_to_all(
        produced.reshape(experts_all, groups_here, D),
        "tensor",
        split_axis=0,
        concat_axis=0,
        tiled=True,
    )
    spread = jnp.einsum("ngse,egd->ngsd", mixing_low, returned, preferred_element_type=jnp.float32)
    back_rows = lax.all_to_all(
        spread.reshape(tok_rows, D).astype(jnp.bfloat16),
        "dp",
        split_axis=0,
        concat_axis=0,
        tiled=True,
    )
    block_out = (residual_one + back_rows[slot_row].astype(jnp.float32)).astype(jnp.bfloat16)
    grad_produced = jnp.einsum(
        "ngse,ngsd->egd", mixing_low, grad_update, preferred_element_type=jnp.float32
    ).astype(jnp.bfloat16)
    grad_mixing = jnp.einsum(
        "ngsd,egd->ngse", grad_update, returned, preferred_element_type=jnp.float32
    )
    expert_grads = lax.all_to_all(grad_produced, "tensor", split_axis=0, concat_axis=0, tiled=True)
    expert_grads = expert_grads.reshape(tensor_size, experts_here, groups_here, D)
    grad_act = jnp.einsum(
        "tegd,efd->tegf", expert_grads, expert_out, preferred_element_type=jnp.float32
    )
    gelu_value, gelu_back = jax.vjp(partial(jax.nn.gelu, approximate=True), pre_act)
    grad_pre = gelu_back(grad_act)[0].astype(jnp.bfloat16)
    grad_mixed = jnp.einsum(
        "tegf,edf->tegd", grad_pre, expert_in, preferred_element_type=jnp.float32
    ).astype(jnp.bfloat16)
    local_in = jnp.einsum(
        "tegd,tegf->edf", expert_rows, grad_pre, preferred_element_type=jnp.float32
    )
    local_out = jnp.einsum(
        "tegf,tegd->efd", activated, expert_grads, preferred_element_type=jnp.float32
    )
    grad_mixed_all = lax.all_to_all(
        grad_mixed.reshape(experts_all, groups_here, D),
        "tensor",
        split_axis=0,
        concat_axis=0,
        tiled=True,
    )
    grad_mixing = grad_mixing + jnp.einsum(
        "egd,ngsd->ngse", grad_mixed_all, members, preferred_element_type=jnp.float32
    )
    grad_member = jnp.einsum(
        "ngse,egd->ngsd", mixing_low, grad_mixed_all, preferred_element_type=jnp.float32
    )
    inner_sum = jnp.sum(mixing * grad_mixing, axis=(0, 2), keepdims=True)
    grad_logits = (mixing * (grad_mixing - inner_sum)).astype(jnp.bfloat16)
    router_part = jnp.einsum(
        "ngsd,ngse->de", members, grad_logits, preferred_element_type=jnp.float32
    )
    grad_member = grad_member + jnp.einsum(
        "ngse,de->ngsd", grad_logits, router_weight, preferred_element_type=jnp.float32
    )
    grad_sorted = lax.all_to_all(
        grad_member.reshape(tok_rows, D).astype(jnp.bfloat16),
        "dp",
        split_axis=0,
        concat_axis=0,
        tiled=True,
    )
    grad_hidden_two = grad_sorted[slot_row].astype(jnp.float32)
    gain_two_part = jnp.sum(grad_hidden_two * normed_two, axis=0)
    grad_residual = cotangent.astype(jnp.float32) + norm_back(
        grad_hidden_two, normed_two, scale_two, norm2_gain
    )
    grad_rows = lax.all_gather(grad_residual.astype(jnp.bfloat16), "tensor", axis=0, tiled=True)
    grad_attn_out = lax.dot_general(
        att_own, grad_rows, contract_first, preferred_element_type=jnp.float32
    )
    grad_attended = lax.dot_general(
        grad_rows, out_weight, contract_last, preferred_element_type=jnp.float32
    )
    grad_attended = grad_attended.astype(jnp.bfloat16)
    first_half = (jnp.arange(128) < 64)[None]
    do2 = jnp.stack((jnp.where(first_half, grad_attended, 0), jnp.where(first_half, 0, grad_attended)))
    delta = jnp.sum(
        (grad_attended.astype(f32) * att_own.astype(f32)).reshape(LENGTH, 2, 64), axis=-1
    ).T
    dq_t, dk, dv = back(doc_lengths, q2, k, k2t, v, do2, delta, lse)
    heads = lambda x: x.reshape(LENGTH, 2, 64)
    grad_projected = jnp.stack((heads(dq_t.T), heads(dk), heads(dv)), axis=2)
    grad_projected = grad_projected.reshape(LENGTH, 384).astype(jnp.bfloat16)
    grad_qkv_part = lax.dot_general(
        rows_one, grad_projected, contract_first, preferred_element_type=jnp.float32
    )
    grad_hidden_one = lax.psum_scatter(
        lax.dot_general(
            grad_projected, qkv_weight, contract_last, preferred_element_type=jnp.float32
        ).astype(jnp.bfloat16),
        "tensor",
        scatter_dimension=0,
        tiled=True,
    ).astype(jnp.float32)
    gain_one_part = jnp.sum(grad_hidden_one * normed_one, axis=0)
    grad_tokens = (
        grad_residual + norm_back(grad_hidden_one, normed_one, scale_one, norm1_gain)
    ).astype(jnp.bfloat16)
    grad_norm1, grad_norm2, grad_router = lax.psum(
        (gain_one_part, gain_two_part, router_part), ("dp", "tensor")
    )
    weight_terms = (grad_qkv_part, grad_attn_out, local_in, local_out)
    summed = tuple(lax.psum(w.astype(bf16), "dp").astype(f32) for w in weight_terms)
    return (
        block_out,
        grad_tokens,
        grad_norm1,
        summed[0],
        summed[1],
        grad_norm2,
        grad_router,
        summed[2],
        summed[3],
    )


def solution(mesh):
    in_specs = (
        P(("dp", "tensor"), None),
        P(("dp", "tensor"), None),
        P("dp", None),
        P(("dp", "tensor"), None),
        P(),
        P(None, "tensor"),
        P("tensor", None),
        P(),
        P(),
        P("tensor", None, None),
        P("tensor", None, None),
    )
    out_specs = (
        P(("dp", "tensor"), None),
        P(("dp", "tensor"), None),
        P(),
        P(None, "tensor"),
        P("tensor", None),
        P(),
        P(),
        P("tensor", None, None),
        P("tensor", None, None),
    )
    return jax.shard_map(local, mesh=mesh, in_specs=in_specs, out_specs=out_specs, check_vma=False)
```

time: 1000 us -> 699 us (0.70)
  matrix products: 248 us -> 31.9 us
  waiting for transfers between devices: 174 us -> 75.1 us
  Pallas kernels: 0 us -> 80.7 us
  local copies, waits for them, and re-layouts: 54.7 us -> 18.1 us
  other arithmetic: 54.2 us -> 30.6 us
  blocking collectives: 387 us -> 408 us
  loops' own time: 16.4 us -> 0 us
  starting transfers between devices: 40.9 us -> 30.4 us
    dot_general x31 -> x1, matrix products: 208 us -> 1.13 us  [local(): lax.dot_general(att_own, grad_rows, contract_first, preferred_element_typ...]
    pallas_call x0 -> x2, Pallas kernels: none -> 80.7 us  [the longest x1 58.6 us: front(): pl.pallas_call(front_kernel, name='front', out_shape=(sds((ROWS, D), bf16...]
    all_gather x1 -> x0, waiting for transfers between devices: 30.6 us -> none  [local(): rows_one = lax.all_gather(hidden_one, 'tensor', axis=0, tiled=True)]
    reduce_scatter x1 -> x0, waiting for transfers between devices: 26.9 us -> none  [local(): lax.psum_scatter(jnp.dot(attn_low, out_weight, preferred_element_type=jnp...]
    psum x1, blocking collectives: 387 us -> 408 us  [local(): lax.psum((gain_one_part, gain_two_part, router_part), ('dp', 'tensor'))]
    psum x1, waiting for transfers between devices: 36 us -> 14.5 us  [local(): lax.psum(w.astype(bf16), 'dp').astype(f32)]
    all_to_all x2 -> x0, waiting for transfers between devices: 21.6 us -> none  [the longest x1 11.4 us: local(): lax.all_to_all(hidden_two[inverse_order], 'dp', split_axis=0, concat_axis...]
    while x40 -> x0, local copies, waits for them, and re-layouts: 17.5 us -> none
  transfers between devices with their start and end apart: 13 -> 9, of which waited for: 10 -> 6; matrix products, arithmetic and copies ran while one was open for 5% -> 5% of each run, Pallas kernels for 0% -> 0%
where the time goes in v1:
time: 699 us; the launch traced here: 690 us
  blocking collectives  408 us (58%)
  Pallas kernels  80.7 us (12%)
  waiting for transfers between devices  75.1 us (11%)
  matrix products  31.9 us (5%)
  other arithmetic  30.6 us (4%)
  starting transfers between devices  30.4 us (4%)
  local copies, waits for them, and re-layouts  18.1 us (3%)
  between operations  14.6 us (2%)
    psum x1, blocking collectives, local(): lax.psum((gain_one_part, gain_two_part, router_part), ('dp', 'tensor'))  408 us
    pallas_call x1, Pallas kernels, front(): pl.pallas_call(front_kernel, name='front', out_shape=(sds((ROWS, D), bf16...  58.6 us
    all_gather x1, waiting for transfers between devices, local(): lax.all_gather(grad_residual.astype(jnp.bfloat16), 'tensor', axis=0, tile...  23.9 us
    pallas_call x1, Pallas kernels, back(): pl.pallas_call(back_kernel, name='attention_back', out_shape=(sds((128, L...  22.1 us
    all_to_all x1, waiting for transfers between devices, local(): lax.all_to_all(spread.reshape(tok_rows, D).astype(jnp.bfloat16), 'dp', sp...  17.1 us
    convert_element_type x4, other arithmetic, local(): lax.psum(w.astype(bf16), 'dp').astype(f32)  15 us
    psum x1, waiting for transfers between devices, local(): lax.psum(w.astype(bf16), 'dp').astype(f32)  14.5 us
  transfers between devices with their start and end apart: 9, of which 6 were waited for; matrix products, arithmetic and copies ran while one was open for 5% of the time, Pallas kernels for 0%

profile of v1, /device:TPU:0, one launch (start us, length us, event | category | flops | bytes accessed | tf_op | source)
XLA Modules:
  0.0 689.8 jit_solution(267172032143945949)
XLA Ops:
  7.2 58.6 %front.1 = (bf16[512,512]{1,0:T(8,128)(2,1)}, bf16[512,512]{1,0:T(8,128)(2,1)}, f32[512,512]{1,0:T(8,128)}, bf16[2048,512]{1,0:T(8,128)(2,1)}, bf16[2,2048,128]{...) custom-call(s32[1,9]{1,0:T(1,128)} %lengths.3, ...), custom_call_target="tpu_custom_call" | custom-call | tf_op jit(solution)/shard_map/front/pallas_call | solution.py:309
  70.0 3.5 all-to-all-start
  74.6 3.5 all-to-all-done
  78.1 3.3 all-to-all-start.3
  81.4 3.2 fusion.11
  86.4 3.3 all-to-all-start.1
  89.8 3.8 fusion.53
  95.7 3.3 all-to-all-start.4
  100.6 3.0 all-to-all-done.4
  106.2 6.9 %all-to-all-start.5 = ((bf16[32,16,512]{2,1,0:T(8,128)(2,1)}), bf16[32,16,512]{2,1,0:T(8,128)(2,1)S(1)}, u32[]{:S(2)}, u32[]{:S(2)}) async-start(bf16[32,16,512]{2,1,0:T(8,128)(2,1)} %copy.115), calls=%async_computation.5 | async-start | bytes 1048576 | tf_op jit(solution)/shard_map/all_to_all | solution.py:528
  113.4 13.2 %all-to-all-done.5 = bf16[32,16,512]{2,1,0:T(8,128)(2,1)S(1)} async-done(((bf16[32,16,512]{2,1,0:T(8,128)(2,1)}), bf16[32,16,512]{2,1,0:T(8,128)(2,1)S(1)}, u32[]{:S(2)}, u32[]{:S(2)}) %all-to-all-start.5) | async-done | bytes 524320 | tf_op jit(solution)/shard_map/all_to_all | solution.py:528
  131.5 23.9 %all-gather.2.cloned.1.call-done = bf16[2048,512]{1,0:T(8,128)(2,1)} async-done(((bf16[512,512]{1,0:T(8,128)(2,1)}), bf16[2048,512]{1,0:T(8,128)(2,1)}) %all-gather.2.cloned.1.call-update) | async-done | bytes 2097168 | tf_op jit(solution)/shard_map/all_gather | solution.py:540
  155.4 3.4 convert_multiply_fusion.6
  164.3 22.1 %attention_back.1 = (f32[128,2048]{1,0:T(8,128)}, f32[2048,128]{1,0:T(8,128)}, f32[2048,128]{1,0:T(8,128)}) custom-call(s32[1,9]{1,0:T(1,128)} %lengths.3, bf16[2,2048,128]{2,1,0:T(8,128)(2,1)} %get-tuple-element.25.q2, bf16[2048,128]{1,0:T(8,128)(2,1)} %get-tuple-element.26.k, bf16[2,128,2048]{2,1,0:T(8,128)(2,1)} %get-tuple-element.27.k2t, ...), custom_call_target="tpu_custom_call" | custom-call | tf_op jit(solution)/shard_map/attention_back/pallas_call | solution.py:391
  194.9 2.7 convolution_convert_fusion
  198.6 3.3 bitcast_convert_fusion.1
  202.0 3.3 bitcast_convert_fusion
  211.1 9.4 %all-to-all-start.2 = ((bf16[32,16,512]{2,1,0:T(8,128)(2,1)}), bf16[32,16,512]{2,1,0:T(8,128)(2,1)S(1)}, u32[]{:S(2)}, u32[]{:S(2)}) async-start(bf16[32,16,512]{2,1,0:T(8,128)(2,1)} %copy.100), calls=%async_computation.2 | async-start | bytes 1048576 | tf_op jit(solution)/shard_map/all_to_all | solution.py:477
  220.9 17.1 %all-to-all-done.2 = bf16[32,16,512]{2,1,0:T(8,128)(2,1)S(1)} async-done(((bf16[32,16,512]{2,1,0:T(8,128)(2,1)}), bf16[32,16,512]{2,1,0:T(8,128)(2,1)S(1)}, u32[]{:S(2)}, u32[]{:S(2)}) %all-to-all-start.2) | async-done | bytes 524320 | tf_op jit(solution)/shard_map/all_to_all | solution.py:477
  242.2 408.4 %all-reduce = (f32[512]{0:T(512)}, f32[512]{0:T(512)}, f32[512,8]{0,1:T(8,128)}) all-reduce(f32[512]{0:T(512)S(1)} %get-tuple-element.37, f32[512]{0:T(512)S(1)} %get-tuple-element.35, f32[512,8]{0,1:T(8,128)S(1)} %convolution_bitcast_fusion.2), channel_id=1, replica_groups=mesh['dp'=32,'tensor'=4] {'dp','tensor'}, use_global_device_ids=true, to_apply=%region_10.11 | all-reduce | flops 5120 | bytes 40960 | tf_op jit(solution)/shard_map/psum | solution.py:572
  650.6 2.8 fusion.39
  653.4 14.5 %all-reduce.4.cloned.1.call-done = (bf16[512,384]{1,0:T(8,128)(2,1)}, bf16[128,512]{1,0:T(8,128)(2,1)}, bf16[2,512,2048]{2,1,0:T(8,128)(2,1)}, bf16[2,2048,512]{2,1,0:T(8,128)(2,1)}) async-done(((bf16[512,384]{1,0:T(8,128)(2,1)}, bf16[128,512]{1,0:T(8,128)(2,1)}, bf16[2,512,2048]{2,1,0:T(8,128)(2,1)}, bf16[2,2048,512]{2,1,0:T(8,128)(2,1)}), (bf16[512,384]{1,0:T(8,128)(2,1)}, bf16[128,512]{1,0:T(8,128)(2,1)}, ...) | async-done | bytes 8912912 | tf_op jit(solution)/shard_map/psum | solution.py:576
  671.5 6.8 convert_element_type.161
  678.3 4.6 convert_element_type.163
  (119 shorter events, 47.4 us)
Async XLA Ops:
  7.2 58.6 %copy-start = (bf16[512,8]{0,1:T(8,128)(2,1)S(1)}, bf16[512,8]{0,1:T(8,128)(2,1)}, u32[]{:S(2)}) copy-start(bf16[512,8]{0,1:T(8,128)(2,1)} %param.19) | copy-start | bytes 24580
  65.8 7.7 %copy-start.27 = (bf16[512,512]{1,0:T(8,128)(2,1)S(1)}, bf16[512,512]{1,0:T(8,128)(2,1)}, u32[]{:S(2)}) copy-start(bf16[512,512]{1,0:T(8,128)(2,1)} %get-tuple-element.24) | copy-start | bytes 1572868
  70.0 8.1 %all-to-all-start = ((bf16[8,16,512]{2,1,0:T(8,128)(2,1)}), bf16[8,16,512]{2,1,0:T(8,128)(2,1)S(1)}, u32[]{:S(2)}, u32[]{:S(2)}) async-start(bf16[8,16,512]{2,1,0:T(8,128)(2,1)} %copy.95), calls=%async_computation | async-start | bytes 262144 | tf_op jit(solution)/shard_map/all_to_all | solution.py:460
  78.1 8.3 %all-to-all-start.3 = ((bf16[8,16,512]{2,1,0:T(8,128)(2,1)}), bf16[8,16,512]{2,1,0:T(8,128)(2,1)S(1)}, u32[]{:S(2)}, u32[]{:S(2)}) async-start(bf16[8,16,512]{2,1,0:T(8,128)(2,1)} %copy.103), calls=%async_computation.3 | async-start | bytes 262144 | tf_op jit(solution)/shard_map/all_to_all | solution.py:491
  86.4 9.3 %all-to-all-start.1 = ((bf16[8,16,512]{2,1,0:T(8,128)(2,1)}), bf16[8,16,512]{2,1,0:T(8,128)(2,1)S(1)}, u32[]{:S(2)}, u32[]{:S(2)}) async-start(bf16[8,16,512]{2,1,0:T(8,128)(2,1)} %bitcast.12), calls=%async_computation.1 | async-start | bytes 262144 | tf_op jit(solution)/shard_map/all_to_all | solution.py:469
  89.7 3.8 copy-start.2
  93.6 10.0 %copy-start.9 = (bf16[512,512]{1,0:T(8,128)(2,1)S(1)}, bf16[512,512]{1,0:T(8,128)(2,1)}, u32[]{:S(2)}) copy-start(bf16[512,512]{1,0:T(8,128)(2,1)} %get-tuple-element.23) | copy-start | bytes 1572868
  95.7 8.8 %copy-start.18 = (bf16[8,16,512]{2,1,0:T(8,128)(2,1)}, bf16[8,16,512]{2,1,0:T(8,128)(2,1)S(1)}, u32[]{:S(2)}) copy-start(bf16[8,16,512]{2,1,0:T(8,128)(2,1)S(1)} %all-to-all-done.1) | copy-start | bytes 393220
  95.7 7.9 %all-to-all-start.4 = ((bf16[8,16,512]{2,1,0:T(8,128)(2,1)}), bf16[8,16,512]{2,1,0:T(8,128)(2,1)S(1)}, u32[]{:S(2)}, u32[]{:S(2)}) async-start(bf16[8,16,512]{2,1,0:T(8,128)(2,1)} %bitcast.26), calls=%async_computation.4 | async-start | bytes 262144 | tf_op jit(solution)/shard_map/all_to_all | solution.py:507
  104.8 8.4 %copy-start.25 = (s32[1,512]{1,0:T(1,128)S(1)}, s32[1,512]{1,0:T(1,128)}, u32[]{:S(2)}) copy-start(s32[1,512]{1,0:T(1,128)} %slot.1) | copy-start | bytes 6148
  104.8 8.4 %copy-start.3 = (f32[512,512]{1,0:T(8,128)S(1)}, f32[512,512]{1,0:T(8,128)}, u32[]{:S(2)}) copy-start(f32[512,512]{1,0:T(8,128)} %get-tuple-element.22) | copy-start | bytes 3145732
  106.2 20.3 %all-to-all-start.5 = ((bf16[32,16,512]{2,1,0:T(8,128)(2,1)}), bf16[32,16,512]{2,1,0:T(8,128)(2,1)S(1)}, u32[]{:S(2)}, u32[]{:S(2)}) async-start(bf16[32,16,512]{2,1,0:T(8,128)(2,1)} %copy.115), calls=%async_computation.5 | async-start | bytes 1048576 | tf_op jit(solution)/shard_map/all_to_all | solution.py:528
  113.1 42.2 %all-gather.2.cloned.1.call-start = ((), (), s32[]{:S(2)}) async-start(), calls=%async_computation.7 | async-start | bytes 2621440 | tf_op jit(solution)/shard_map/all_gather | solution.py:540
  128.5 26.8 %copy-start.17 = (bf16[128,512]{1,0:T(8,128)(2,1)S(1)}, bf16[128,512]{1,0:T(8,128)(2,1)}, u32[]{:S(2)}) copy-start(bf16[128,512]{1,0:T(8,128)(2,1)} %out_w.1) | copy-start | bytes 393220
  131.2 109.5 %reduce-scatter.2.cloned.1.call-start = ((), (), s32[]{:S(2)}) async-start(), calls=%async_computation.8 | async-start | bytes 2621440 | tf_op jit(solution)/shard_map/reduce_scatter | solution.py:560
  197.6 4.3 copy-start.22
  197.6 470.3 %all-reduce.4.cloned.1.call-start = ((), (), s32[]{:S(2)}) async-start(), calls=%async_computation.9 | async-start | bytes 17825792 | tf_op jit(solution)/shard_map/psum | solution.py:576
  202.0 4.5 copy-start.26
  209.7 10.8 %copy-start.5 = (bf16[512,512]{1,0:T(8,128)(2,1)S(1)}, bf16[512,512]{1,0:T(8,128)(2,1)}, u32[]{:S(2)}) copy-start(bf16[512,512]{1,0:T(8,128)(2,1)} %tokens.1) | copy-start | bytes 1572868
  209.7 11.0 %copy-start.10 = (bf16[512,512]{1,0:T(8,128)(2,1)S(1)}, bf16[512,512]{1,0:T(8,128)(2,1)}, u32[]{:S(2)}) copy-start(bf16[512,512]{1,0:T(8,128)(2,1)} %get-tuple-element.23) | copy-start | bytes 1572868
  211.1 26.9 %all-to-all-start.2 = ((bf16[32,16,512]{2,1,0:T(8,128)(2,1)}), bf16[32,16,512]{2,1,0:T(8,128)(2,1)S(1)}, u32[]{:S(2)}, u32[]{:S(2)}) async-start(bf16[32,16,512]{2,1,0:T(8,128)(2,1)} %copy.100), calls=%async_computation.2 | async-start | bytes 1048576 | tf_op jit(solution)/shard_map/all_to_all | solution.py:477
  238.0 412.6 %copy-start.6 = (bf16[512,512]{1,0:T(8,128)(2,1)S(1)}, bf16[512,512]{1,0:T(8,128)(2,1)}, u32[]{:S(2)}) copy-start(bf16[512,512]{1,0:T(8,128)(2,1)} %cotangent.1) | copy-start | bytes 1572868
  671.5 6.8 copy-start.7
  678.3 4.6 copy-start.1
  (13 other events, 27.6 us)
Sparse Core Ops, SparseCore 0:
  131.3 24.0 all-gather.1
  197.7 33.1 reduce-scatter.1
  235.1 432.7 all-reduce.3
